TPU v7x, 32 devices: a whole 2x2x4 slice. The times are simulated.
32 devices in a mesh: design: 2 (over y), harm: 4 (over z), tile: 4 (over x, core).
Axes of the slice: x: 2, y: 2, z: 4, core: 2. Of those that a mesh axis runs over, the one named last changes fastest.
Arguments:
- fwd_ckpt: bfloat16 [8, 2, 2, 6, 3, 2624], P(('design', 'tile'), None, None, None, None, 'harm'), parts along dimension 0, as said below
- adj_amp: bfloat16 [4, 2, 6, 3, 2624], P('design', None, None, None, 'harm'), parts along dimension 0, as said below
- layer_owner: int32 [4], P('design'), parts along dimension 0, may hold values from 0 to 3, as said below
- source_list: int32 [12], P('design'), parts along dimension 0, may hold values from 0 to 5, each once
Outputs:
- grad: float32 [4, 8192], P('design', ('harm', 'tile')), parts along dimension 0
There are 2 independent parts, one for each index of `design`. A program takes and returns all parts, laid end to end along the dimension named above; each array names one. Nothing has to cross between parts.
Inputs may be any that keep to these rules, and one draw needn't show every extreme that they name: `layer_owner`: the layers' slots are distinct. `source_list`: each source appears once. `fwd_ckpt`: entries of harmonics 2601 and above are zero. `adj_amp`: entries of harmonics 2601 and above are zero.
All inputs are finite; a program needn't handle non-finite values.
Results may differ from a plain program's by a relative error of at most 0.0034.
Values may be sent and summed in bfloat16 or wider, within the bound.
A program may use at most 64 MiB of HBM per device.

v0:
```python
import math

import jax
import jax.numpy as jnp
from jax import lax
from jax.sharding import PartitionSpec as P

GRID = 512
ORD = 51
PIX_DEV = 512


def from_root(value, axis, source):
    kept = jnp.where(lax.axis_index(axis) == source, value, 0).astype(value.dtype)
    return lax.psum(kept, axis)


def make_basis(count_harm, first_pix, count_pix):
    harmonic = jnp.arange(count_harm, dtype=jnp.int32)
    order_x = harmonic % ORD - ORD // 2
    order_y = harmonic // ORD - ORD // 2
    pixel = first_pix + jnp.arange(count_pix, dtype=jnp.int32)
    column = pixel % GRID
    row_id = pixel // GRID
    phase = jnp.mod(order_x[:, None] * column[None, :] + order_y[:, None] * row_id[None, :], GRID)
    angle = phase.astype(jnp.float32) * jnp.float32(2.0 * math.pi / GRID)
    return jnp.concatenate([jnp.cos(angle), jnp.sin(angle)], axis=0).astype(jnp.bfloat16)


def panel(amp):
    layers = amp.shape[0]
    width = amp.shape[4]
    rows = amp.shape[2] * amp.shape[3]
    real_part = amp[:, 0].reshape(layers, rows, width)
    imag_part = amp[:, 1].reshape(layers, rows, width)
    upper = jnp.concatenate([real_part, -imag_part], axis=2)
    lower = jnp.concatenate([imag_part, real_part], axis=2)
    return jnp.concatenate([upper, lower], axis=1)


def accumulate(fwd_piece, adj_piece, pixel_start):
    count = adj_piece.shape[4]
    fwd_panel = panel(fwd_piece)
    adj_panel = panel(adj_piece)
    step_pix = min(256, PIX_DEV)
    fwd_parts = []
    adj_parts = []
    for offset in range(0, PIX_DEV, step_pix):
        basis = make_basis(count, pixel_start + offset, step_pix)
        fwd_parts.append(
            jnp.einsum("lrk,kp->lrp", fwd_panel, basis, preferred_element_type=jnp.float32)
        )
        adj_parts.append(
            jnp.einsum("lrk,kp->lrp", adj_panel, basis, preferred_element_type=jnp.float32)
        )
    return (jnp.concatenate(fwd_parts, axis=2), jnp.concatenate(adj_parts, axis=2))


def per_device(fwd_ckpt, adj_amp, layer_owner, source_list):
    own_slot = fwd_ckpt[0]
    layers = own_slot.shape[0]
    rows = 3 * own_slot.shape[2]
    pixel_start = (
        lax.axis_index("harm") * lax.axis_size("tile") + lax.axis_index("tile")
    ) * PIX_DEV
    whole = lax.all_gather(own_slot, "harm", axis=4, tiled=True)
    spread = []
    for layer in range(layers):
        spread.append(from_root(whole[layer], "tile", layer_owner[layer]))
    forward = jnp.take(jnp.stack(spread), source_list, axis=2)
    fields = accumulate(forward, lax.all_gather(adj_amp, "harm", axis=4, tiled=True), pixel_start)
    fwd_field = fields[0].reshape(layers, 2, rows, PIX_DEV)
    adj_field = fields[1].reshape(layers, 2, rows, PIX_DEV)
    total = jnp.sum(fwd_field[:, 0] * adj_field[:, 0], axis=1) - jnp.sum(
        fwd_field[:, 1] * adj_field[:, 1], axis=1
    )
    return total * jnp.float32(rows ** (-0.5))


def solution(mesh):
    return jax.shard_map(
        per_device,
        mesh=mesh,
        in_specs=(
            P(("design", "tile"), None, None, None, None, "harm"),
            P("design", None, None, None, "harm"),
            P("design"),
            P("design"),
        ),
        out_specs=P("design", ("harm", "tile")),
        check_vma=False,
    )
```

profile of v0, /device:TPU:0, one launch (start us, length us, event | category | flops | bytes accessed | tf_op | source)
XLA Modules:
  0.0 427.5 jit_solution(15652802301539250476)
XLA Ops:
  6.5 0.0 all-reduce.3.cloned.1.call-start
  6.5 3.9 copy.58
  10.5 135.7 %all-gather = bf16[1,2,2,6,3,2624]{3,2,4,1,0,5:T(2,128)(2,1)S(1)} all-gather(bf16[1,2,2,6,3,656]{3,2,4,1,0,5:T(2,128)(2,1)S(1)} %copy.58), channel_id=2, replica_groups=mesh['design'=2,'harm'=4,'tile'=4] {'harm'}, dimensions={5}, use_global_device_ids=true | all-gather | bytes 472320 | tf_op jit(solution)/shard_map/all_gather | solution.py:66
  146.2 6.7 %fusion.31 = (bf16[1,1,2,6,3,2624]{3,2,4,1,0,5:T(2,128)(2,1)}, bf16[1,1,2,6,3,2624]{3,2,4,1,0,5:T(2,128)(2,1)}) fusion(bf16[1,2,2,6,3,2624]{3,2,4,1,0,5:T(2,128)(2,1)S(1)} %all-gather), kind=kLoop, calls=%fused_computation.81 | loop fusion | bytes 755712 | tf_op jit(solution)/shard_map/slice | solution.py:69
  152.8 12.7 %copy.74 = bf16[1,1,2,6,3,2624]{5,4,2,3,1,0:T(4,128)(2,1)S(1)} copy(bf16[1,1,2,6,3,2624]{3,2,4,1,0,5:T(2,128)(2,1)} %get-tuple-element.10) | data formatting | bytes 377856
  165.5 0.0 copy-done.7
  165.6 0.6 fusion.34
  166.2 12.7 %copy.73 = bf16[1,1,2,6,3,2624]{5,4,2,3,1,0:T(4,128)(2,1)S(1)} copy(bf16[1,1,2,6,3,2624]{3,2,4,1,0,5:T(2,128)(2,1)} %get-tuple-element.9) | data formatting | bytes 377856
  180.3 0.8 select_bitcast_fusion.1
  181.1 0.8 select_bitcast_fusion.2
  181.9 0.0 all-reduce.3.cloned.1.call-update
  182.0 0.0 copy-done.6
  182.0 2.7 copy.67
  184.7 134.2 %all_gather.7 = bf16[2,2,6,3,2624]{2,1,3,0,4:T(2,128)(2,1)S(1)} all-gather(bf16[2,2,6,3,656]{2,1,3,0,4:T(2,128)(2,1)S(1)} %copy.67), channel_id=1, replica_groups=mesh['design'=2,'harm'=4,'tile'=4] {'harm'}, dimensions={4}, use_global_device_ids=true | all-gather | bytes 472320 | tf_op jit(solution)/shard_map/all_gather | solution.py:71
  319.0 12.5 %fusion.32 = (bf16[2,1,6,3,2624]{2,1,3,0,4:T(2,128)(2,1)}, bf16[2,1,6,3,2624]{2,1,3,0,4:T(2,128)(2,1)}) fusion(bf16[2,2,6,3,2624]{2,1,3,0,4:T(2,128)(2,1)S(1)} %all_gather.7), kind=kLoop, calls=%fused_computation.82 | loop fusion | bytes 755712 | tf_op jit(solution)/shard_map/slice | solution.py:35
  331.5 18.7 %copy.68 = bf16[2,1,6,3,2624]{4,0,3,2,1:T(2,128)(2,1)S(1)} copy(bf16[2,1,6,3,2624]{2,1,3,0,4:T(2,128)(2,1)} %get-tuple-element.12) | data formatting | bytes 377856 | tf_op jit(solution)/shard_map/slice | solution.py:34
  350.1 18.7 %copy.69 = bf16[2,1,6,3,2624]{4,0,3,2,1:T(2,128)(2,1)S(1)} copy(bf16[2,1,6,3,2624]{2,1,3,0,4:T(2,128)(2,1)} %get-tuple-element.11) | data formatting | bytes 377856 | tf_op jit(solution)/shard_map/slice | solution.py:35
  368.8 0.2 bitcast_negate_fusion
  369.0 9.5 %fusion.14 = bf16[2,36,5248]{2,0,1:T(2,128)(2,1)S(1)} fusion(bf16[2,18,2624]{2,0,1:T(2,128)(2,1)S(1)} %bitcast.27, bf16[2,18,2624]{2,0,1:T(2,128)(2,1)S(1)} %bitcast.25, bf16[2,18,2624]{2,0,1:T(2,128)(2,1)S(1)} %bitcast_negate_fusion), kind=kLoop, calls=%fused_computation.28 | loop fusion | flops 3022848 | bytes 1322496 | tf_op jit(solution)/shard_map/concatenate | solution.py:38
  378.6 23.5 %cosine_convert_fusion.1 = (bf16[2624,256]{1,0:T(8,128)(2,1)S(1)}, bf16[2624,256]{1,0:T(8,128)(2,1)S(1)}, bf16[2624,256]{1,0:T(8,128)(2,1)S(1)}, bf16[2624,256]{1,0:T(8,128)(2,1)S(1)}) fusion(s32[256]{0:T(256)S(1)} %get-tuple-element.23, s32[2624]{0:T(1024)S(1)} %get-tuple-element.27, s32[256]{0:T(256)S(1)} %get-tuple-element.24, ...), kind=kLoop, calls=%fused_computation.18 | loop fusion | flops 24182784 | bytes 5399040 | tf_op jit(solution)/shard_map/convert.2
  402.1 0.0 copy-start.2
  402.1 0.0 copy-start.4
  402.1 0.0 copy-start
  402.1 0.6 fusion.6
  402.7 0.4 copy-done.2
  403.1 0.4 copy-done.4
  403.6 0.4 copy-done
  404.0 0.6 fusion.8
  404.6 0.1 copy.72
  404.7 0.0 copy-done.8
  404.8 0.0 all-reduce.3.cloned.1.call-done
  404.8 1.4 pad_maximum_fusion.4
  406.2 1.0 gather_fusion
  407.2 0.0 copy-start.3
  407.2 0.0 copy-start.5
  407.3 0.3 select_bitcast_fusion
  407.5 0.2 fusion.33
  407.7 0.2 copy.62
  407.9 0.2 copy.63
  408.1 0.2 bitcast_negate_fusion.1
  408.3 9.5 %fusion.15 = bf16[2,36,5248]{2,0,1:T(2,128)(2,1)S(1)} fusion(bf16[2,18,2624]{2,0,1:T(2,128)(2,1)S(1)} %bitcast.28, bf16[2,18,2624]{2,0,1:T(2,128)(2,1)S(1)} %bitcast.26, bf16[2,18,2624]{2,0,1:T(2,128)(2,1)S(1)} %bitcast_negate_fusion.1), kind=kLoop, calls=%fused_computation.31 | loop fusion | flops 3022848 | bytes 1322496 | tf_op jit(solution)/shard_map/concatenate | solution.py:38
  417.8 0.0 copy-done.3
  417.8 0.6 fusion.7
  418.5 0.7 copy-done.1
  419.2 0.6 fusion.9
  419.8 0.1 copy.66
  419.9 0.1 fusion.16
  420.1 0.6 subtract_multiply_fusion
  (13 shorter events, 0.1 us)
Async XLA Ops:
  6.5 398.3 %all-reduce.3.cloned.1.call-start = ((), (), s32[]{:S(2)}) async-start(), calls=%async_computation | async-start | bytes 1032192 | tf_op jit(solution)/shard_map/psum | solution.py:15
  152.8 12.7 %copy-start.7 = (s32[2]{0:T(128)S(1)}, s32[2]{0:T(128)}, u32[]{:S(2)}) copy-start(s32[2]{0:T(128)} %param.6) | copy-start | bytes 28
  166.2 15.8 %copy-start.6 = (bf16[2,2,6,3,656]{4,1,3,2,0:T(2,128)(2,1)S(1)}, bf16[2,2,6,3,656]{4,1,3,2,0:T(2,128)(2,1)}, u32[]{:S(2)}) copy-start(bf16[2,2,6,3,656]{4,1,3,2,0:T(2,128)(2,1)} %param.5) | copy-start | bytes 283396
  402.1 1.1 copy-start.2
  402.1 1.5 copy-start.4
  402.1 1.9 copy-start
  404.0 0.8 copy-start.8
  407.2 10.6 %copy-start.3 = (bf16[2624,256]{1,0:T(8,128)(2,1)S(1)}, bf16[2624,256]{1,0:T(8,128)(2,1)}, u32[]{:S(2)}) copy-start(bf16[2624,256]{1,0:T(8,128)(2,1)} %copy-done.2) | copy-start | bytes 4030468
  407.2 10.6 %copy-start.5 = (bf16[2624,256]{1,0:T(8,128)(2,1)S(1)}, bf16[2624,256]{1,0:T(8,128)(2,1)}, u32[]{:S(2)}) copy-start(bf16[2624,256]{1,0:T(8,128)(2,1)} %copy-done.4) | copy-start | bytes 4030468
  417.8 1.3 copy-start.1
Sparse Core Ops, SparseCore 0:
  182.1 35.0 all-reduce.2
where the time goes:
time: 429 us; the launch traced here: 428 us
  blocking collectives  270 us (63%)
  local copies, waits for them, and re-layouts  93 us (22%)
  other arithmetic  47.1 us (11%)
  between operations  15 us (3%)
    all_gather x1, blocking collectives, per_device(): whole = lax.all_gather(own_slot, 'harm', axis=4, tiled=True)  136 us
    all_gather x1, blocking collectives, per_device(): lax.all_gather(adj_amp, 'harm', axis=4, tiled=True)  134 us
    unnamed x22, local copies, waits for them, and re-layouts  34.1 us
    slice x4, local copies, waits for them, and re-layouts, panel(): imag_part = amp[:, 1].reshape(layers, rows, width)  31.5 us
    another operation x1, other arithmetic  23.5 us
    concatenate x2, other arithmetic, panel(): return jnp.concatenate([upper, lower], axis=1)  19.1 us
    slice x2, local copies, waits for them, and re-layouts, panel(): real_part = amp[:, 0].reshape(layers, rows, width)  18.8 us
  transfers between devices with their start and end apart: 1, of which 0 were waited for; matrix products, arithmetic and copies ran while one was open for 20% of the time, Pallas kernels for 0%

commit v1 on v0

v1 whole, which is shorter than its diff:
```python
import functools
import math

import jax
import jax.numpy as jnp
import ml_dtypes
import numpy as np
from jax import lax
from jax.experimental import pallas as pl
from jax.experimental.pallas import tpu as pltpu
from jax.sharding import PartitionSpec as P

GRID = 512
ORD = 51
HALF = 64
LANES = 128
ROWS = 24
MESH = pl.DeviceIdType.MESH


def split(value):
    high = value.astype(ml_dtypes.bfloat16)
    low = (value - high.astype(value.dtype)).astype(ml_dtypes.bfloat16)
    return high, low


def make_tables(n_harm, n_tile, depth, wide):
    harmonic = np.arange(n_harm * depth).reshape(n_harm, depth)
    order_y = harmonic // ORD - ORD // 2
    place_x = harmonic % ORD
    row_id = np.arange(n_harm * n_tile)
    angle = (order_y[:, None, :] * row_id[None, :, None] % GRID) * (2.0 * math.pi / GRID)
    twiddle = np.zeros((n_harm, n_harm * n_tile, 2, wide), np.float32)
    twiddle[:, :, 0, :depth] = np.cos(angle)
    twiddle[:, :, 1, :depth] = np.sin(angle)
    pick = np.zeros((n_harm, wide, LANES), ml_dtypes.bfloat16)
    lane = np.arange(LANES) % HALF
    pick[:, :depth, :] = place_x[:, :, None] == lane[None, None, :]
    order_x = np.arange(ORD) - ORD // 2
    angle = (order_x[:, None] * np.arange(GRID)[None, :] % GRID) * (2.0 * math.pi / GRID)
    column = np.zeros((LANES, 2 * GRID), np.float32)
    column[:ORD, :GRID] = np.cos(angle)
    column[HALF : HALF + ORD, :GRID] = -np.sin(angle)
    column[:ORD, GRID:] = np.sin(angle)
    column[HALF : HALF + ORD, GRID:] = np.cos(angle)
    return twiddle, pick, np.stack(split(column))


def kernel(
    n_harm, n_tile, fwd_ref, adj_ref, owner_ref, source_ref, twiddle_hbm, pick_hbm, column_hbm,
    out_ref, twiddle, pick, column, amp, left, send_f, send_a, recv_f, recv_a,
    load_sem, sent_f, sent_a, got_f, got_a,
):
    layers, _, sources, comps, depth = adj_ref.shape
    n_dev = n_harm * n_tile
    wide = amp.shape[-1]
    harm = lax.axis_index("harm")
    tile = lax.axis_index("tile")
    me = harm * n_tile + tile

    loads = [
        pltpu.make_async_copy(twiddle_hbm.at[harm], twiddle, load_sem.at[0]),
        pltpu.make_async_copy(pick_hbm.at[harm], pick, load_sem.at[1]),
        pltpu.make_async_copy(column_hbm, column, load_sem.at[2]),
    ]
    for load in loads:
        load.start()

    def peer(step):
        other = lax.rem(me + step, n_dev)
        return other, {"harm": other // n_tile, "tile": lax.rem(other, n_tile)}

    barrier = pltpu.get_barrier_semaphore()

    def greet(step, carry):
        pl.semaphore_signal(barrier, inc=1, device_id=peer(step)[1], device_id_type=MESH)
        return carry

    lax.fori_loop(1, n_dev, greet, 0)

    amp[...] = jnp.zeros_like(amp)
    mine = jnp.int32(0)
    for layer in range(1, layers):
        mine = jnp.where(owner_ref[layer] == tile, layer, mine)
    for part in range(2):
        for source in range(sources):
            rows = slice(source * comps, source * comps + comps)
            amp[0, part, rows, :depth] = fwd_ref[0, mine, part, source_ref[source]].astype(jnp.float32)
            for layer in range(layers):
                amp[1 + layer, part, rows, :depth] = adj_ref[layer, part, source].astype(jnp.float32)
    loads[0].wait()
    loads[1].wait()

    low_lanes = lax.broadcasted_iota(jnp.int32, (ROWS, LANES), 1) < HALF

    def stage(group, row_id, slot):
        cosine = twiddle[row_id, 0:1, :]
        sine = twiddle[row_id, 1:2, :]
        real, imag = amp[group, 0], amp[group, 1]
        turned = jnp.concatenate(
            [real * cosine - imag * sine, real * sine + imag * cosine], axis=0
        )
        high = turned.astype(jnp.bfloat16)
        rows = slice(slot * 2 * ROWS, (slot + 1) * 2 * ROWS)
        left[0, rows, :] = high
        left[1, rows, :] = (turned - high.astype(jnp.float32)).astype(jnp.bfloat16)

    def partial_sums(to_harm):
        for to_tile in range(n_tile):
            stage(0, to_harm * n_tile + to_tile, to_tile)
        for layer in range(layers):
            stage(1 + layer, to_harm * n_tile + tile, n_tile + layer)
        right = pick[...]
        sums = jnp.dot(left[0], right, preferred_element_type=jnp.float32) + jnp.dot(
            left[1], right, preferred_element_type=jnp.float32
        )
        packed = []
        for slot in range(n_tile + layers):
            start = slot * 2 * ROWS
            packed.append(
                jnp.where(low_lanes, sums[start : start + ROWS], sums[start + ROWS : start + 2 * ROWS])
            )
        return packed[:n_tile], packed[n_tile:]

    def copy_f(to_harm, to_tile, slot):
        return pltpu.make_async_remote_copy(
            src_ref=send_f.at[to_harm * n_tile + to_tile],
            dst_ref=recv_f.at[slot],
            send_sem=sent_f.at[to_harm * n_tile + to_tile],
            recv_sem=got_f.at[slot],
            device_id={"harm": to_harm, "tile": to_tile},
            device_id_type=MESH,
        )

    def copy_a(to_harm, slot):
        return pltpu.make_async_remote_copy(
            src_ref=send_a.at[to_harm],
            dst_ref=recv_a.at[slot],
            send_sem=sent_a.at[to_harm],
            recv_sem=got_a.at[slot],
            device_id={"harm": to_harm, "tile": tile},
            device_id_type=MESH,
        )

    def compute(to_harm):
        fwd, adj = partial_sums(to_harm)
        for to_tile in range(n_tile):
            send_f[to_harm * n_tile + to_tile] = fwd[to_tile]
        send_a[to_harm] = jnp.concatenate(adj, axis=0)

    def block(step):
        to_harm = lax.rem(harm + step, n_harm)
        compute(to_harm)
        return to_harm

    def send_block(to_harm):
        for to_tile in range(n_tile):
            copy_f(to_harm, to_tile, me).start()
        copy_a(to_harm, harm).start()

    first = block(1)
    pl.semaphore_wait(barrier, n_dev - 1)
    send_block(first)

    def away(step, carry):
        send_block(block(step))
        return carry

    lax.fori_loop(2, n_harm, away, 0)

    compute(harm)
    for step in range(1, n_tile):
        copy_f(harm, lax.rem(tile + step, n_tile), me).start()
    recv_f[me] = send_f[me]
    recv_a[harm] = send_a[harm]
    loads[2].wait()

    def arrive_f(step, carry):
        other, _ = peer(step)
        copy_f(other // n_tile, lax.rem(other, n_tile), other).wait()
        return carry

    def arrive_a(step, carry):
        other = lax.rem(harm + step, n_harm)
        copy_a(other, other).wait()
        return carry

    lax.fori_loop(1, n_dev, arrive_f, 0)
    lax.fori_loop(1, n_harm, arrive_a, 0)

    def add_f(layer):
        owner = owner_ref[layer]
        return lax.fori_loop(
            0,
            n_harm,
            lambda source, total: total + recv_f[source * n_tile + owner],
            jnp.zeros((ROWS, LANES), jnp.float32),
        )

    adj = lax.fori_loop(
        0,
        n_harm,
        lambda source, total: total + recv_a[source],
        jnp.zeros((layers * ROWS, LANES), jnp.float32),
    )
    lines = jnp.concatenate([add_f(layer) for layer in range(layers)] + [adj], axis=0)
    high = lines.astype(jnp.bfloat16)
    low = (lines - high.astype(jnp.float32)).astype(jnp.bfloat16)
    fields = (
        jnp.dot(high, column[0], preferred_element_type=jnp.float32)
        + jnp.dot(low, column[0], preferred_element_type=jnp.float32)
        + jnp.dot(high, column[1], preferred_element_type=jnp.float32)
    )
    for layer in range(layers):
        one = fields[layer * ROWS : (layer + 1) * ROWS]
        two = fields[(layers + layer) * ROWS : (layers + layer + 1) * ROWS]
        both = one * two
        out_ref[layer : layer + 1, :] = jnp.sum(
            both[:, :GRID] - both[:, GRID:], axis=0, keepdims=True
        )


def per_device(n_harm, n_tile, fwd_ckpt, adj_amp, layer_owner, source_list):
    layers, _, sources, comps, depth = adj_amp.shape
    assert sources * comps <= ROWS
    wide = -(-depth // LANES) * LANES
    n_dev = n_harm * n_tile
    twiddle, pick, column = make_tables(n_harm, n_tile, depth, wide)
    slots = n_tile + layers
    vmem = pl.BlockSpec(memory_space=pltpu.VMEM)
    smem = pl.BlockSpec(memory_space=pltpu.SMEM)
    hbm = pl.BlockSpec(memory_space=pl.ANY)
    total = pl.pallas_call(
        functools.partial(kernel, n_harm, n_tile),
        out_shape=jax.ShapeDtypeStruct((layers, GRID), jnp.float32),
        in_specs=[vmem, vmem, smem, smem, hbm, hbm, hbm],
        out_specs=vmem,
        scratch_shapes=[
            pltpu.VMEM((n_dev, 2, wide), jnp.float32),
            pltpu.VMEM((wide, LANES), jnp.bfloat16),
            pltpu.VMEM(column.shape, jnp.bfloat16),
            pltpu.VMEM((1 + layers, 2, ROWS, wide), jnp.float32),
            pltpu.VMEM((2, slots * 2 * ROWS, wide), jnp.bfloat16),
            pltpu.VMEM((n_dev, ROWS, LANES), jnp.float32),
            pltpu.VMEM((n_harm, layers * ROWS, LANES), jnp.float32),
            pltpu.VMEM((n_dev, ROWS, LANES), jnp.float32),
            pltpu.VMEM((n_harm, layers * ROWS, LANES), jnp.float32),
            pltpu.SemaphoreType.DMA((3,)),
            pltpu.SemaphoreType.DMA((n_dev,)),
            pltpu.SemaphoreType.DMA((n_harm,)),
            pltpu.SemaphoreType.DMA((n_dev,)),
            pltpu.SemaphoreType.DMA((n_harm,)),
        ],
        compiler_params=pltpu.CompilerParams(
            collective_id=0, has_side_effects=True, vmem_limit_bytes=40 * 1024 * 1024
        ),
    )(
        fwd_ckpt, adj_amp, layer_owner, source_list,
        jnp.asarray(twiddle), jnp.asarray(pick), jnp.asarray(column),
    )
    return total * jnp.float32((sources * comps) ** (-0.5))


def solution(mesh):
    return jax.shard_map(
        functools.partial(per_device, mesh.shape["harm"], mesh.shape["tile"]),
        mesh=mesh,
        in_specs=(
            P(("design", "tile"), None, None, None, None, "harm"),
            P("design", None, None, None, "harm"),
            P("design"),
            P("design"),
        ),
        out_specs=P("design", ("harm", "tile")),
        check_vma=False,
    )
```

time: 429 us -> 19.6 us (0.05)
  blocking collectives: 270 us -> 0 us
  local copies, waits for them, and re-layouts: 93 us -> 4.16 us
  other arithmetic: 47.1 us -> 0.6 us
  between operations: 15 us -> 0.06 us
  Pallas kernels: 0 us -> 14.5 us
    all_gather x2 -> x0, blocking collectives: 270 us -> none  [the longest x1 136 us: per_device(): whole = lax.all_gather(own_slot, 'harm', axis=4, tiled=True)]
    slice x8 -> x0, local copies, waits for them, and re-layouts: 57.7 us -> none  [the longest x4 31.5 us: panel(): imag_part = amp[:, 1].reshape(layers, rows, width)]
    unnamed x22 -> x12, local copies, waits for them, and re-layouts: 34.1 us -> 4.16 us
    another operation x2 -> x0, other arithmetic: 24.9 us -> none
    concatenate x4 -> x0, other arithmetic: 19.1 us -> none  [the longest x2 19.1 us: panel(): return jnp.concatenate([upper, lower], axis=1)]
    pallas_call x0 -> x1, Pallas kernels: none -> 14.5 us  [per_device(): pl.pallas_call(functools.partial(kernel, n_harm, n_tile), out_shape=jax.S...]
  transfers between devices with their start and end apart: 1 -> 0, of which waited for: 0 -> 0; matrix products, arithmetic and copies ran while one was open for 20% -> 0% of each run, Pallas kernels for 0% -> 0%
where the time goes in v1:
time: 19.6 us; the launch traced here: 19.3 us
  Pallas kernels  14.5 us (74%)
  local copies, waits for them, and re-layouts  4.16 us (21%)
  other arithmetic  0.6 us (3%)
    pallas_call x1, Pallas kernels, per_device(): pl.pallas_call(functools.partial(kernel, n_harm, n_tile), out_shape=jax.S...  14.5 us
    unnamed x12, local copies, waits for them, and re-layouts  4.16 us
    mul x1, other arithmetic, per_device(): return total * jnp.float32((sources * comps) ** (-0.5))  0.6 us

profile of v1, /device:TPU:0, one launch (start us, length us, event | category | flops | bytes accessed | tf_op | source)
XLA Modules:
  0.0 19.3 jit_solution(13472012426444745285)
XLA Ops:
  0.0 0.0 copy-start.2
  0.0 1.0 %copy.8.fwd_ref = bf16[1,2,2,6,3,656]{5,4,3,2,1,0:T(4,128)(2,1)S(1)} copy(bf16[1,2,2,6,3,656]{5,2,4,3,1,0:T(2,128)(2,1)} %param.7) | data formatting | bytes 188928 | tf_op args[0]
  1.0 0.0 copy-start.3
  1.0 0.0 copy-start.4
  1.0 1.0 %copy.9.adj_ref = bf16[2,2,6,3,656]{4,3,2,1,0:T(4,128)(2,1)S(1)} copy(bf16[2,2,6,3,656]{4,1,3,2,0:T(2,128)(2,1)} %param.8) | data formatting | bytes 188928 | tf_op args[1]
  2.0 0.0 copy-done.2
  2.0 0.0 copy-done.3
  2.0 0.0 copy-done.4
  2.0 0.0 copy-start
  2.0 1.1 %copy-done = bf16[4,768,128]{2,1,0:T(8,128)(2,1)S(1)} copy-done((bf16[4,768,128]{2,1,0:T(8,128)(2,1)S(1)}, bf16[4,768,128]{2,1,0:T(8,128)(2,1)}, u32[]{:S(2)}) %copy-start) | copy-done | bytes 786456
  3.2 0.0 copy-start.1
  3.2 1.0 %copy-done.1 = bf16[2,128,1024]{2,1,0:T(8,128)(2,1)S(1)} copy-done((bf16[2,128,1024]{2,1,0:T(8,128)(2,1)S(1)}, bf16[2,128,1024]{2,1,0:T(8,128)(2,1)}, u32[]{:S(2)}) %copy-start.1) | copy-done | bytes 524312
  4.2 14.5 %shard_map.73 = f32[2,512]{1,0:T(2,128)S(1)} custom-call(bf16[1,2,2,6,3,656]{5,4,3,2,1,0:T(4,128)(2,1)S(1)} %copy.8.fwd_ref, bf16[2,2,6,3,656]{4,3,2,1,0:T(4,128)(2,1)S(1)} %copy.9.adj_ref, s32[2]{0:T(128)S(1)} %copy-done.3, s32[6]{0:T(128)S(1)} %copy-done.4, f32[4,16,2,768]{3,2,1,0:T(2,128)S(1)} %copy-done.2, bf16[4,768,128]{2,1,0:T(8,128)(2,1)S(1)} %copy-done, ...), custom_call_target="tpu_custom_call" | custom-call | tf_op jit(solution)/shard_map/pallas_call | solution.py:233
  18.7 0.6 %broadcast_multiply_fusion = f32[2,512]{1,0:T(2,128)} fusion(f32[2,512]{1,0:T(2,128)S(1)} %shard_map.73), kind=kLoop, calls=%fused_computation | loop fusion | flops 1024 | bytes 8192 | tf_op jit(solution)/shard_map/mul | solution.py:261
Async XLA Ops:
  0.0 2.0 %copy-start.2 = (f32[4,16,2,768]{3,2,1,0:T(2,128)S(1)}, f32[4,16,2,768]{3,2,1,0:T(2,128)}, u32[]{:S(2)}) copy-start(f32[4,16,2,768]{3,2,1,0:T(2,128)} %constant.8.clone.twiddle_hbm) | copy-start | bytes 1179652
  1.0 1.0 %copy-start.3 = (s32[2]{0:T(128)S(1)}, s32[2]{0:T(128)}, u32[]{:S(2)}) copy-start(s32[2]{0:T(128)} %owner_ref.1) | copy-start | bytes 28
  1.0 1.0 %copy-start.4 = (s32[6]{0:T(128)S(1)}, s32[6]{0:T(128)}, u32[]{:S(2)}) copy-start(s32[6]{0:T(128)} %source_ref.1) | copy-start | bytes 76
  2.0 1.1 %copy-start = (bf16[4,768,128]{2,1,0:T(8,128)(2,1)S(1)}, bf16[4,768,128]{2,1,0:T(8,128)(2,1)}, u32[]{:S(2)}) copy-start(bf16[4,768,128]{2,1,0:T(8,128)(2,1)} %constant.9.clone.pick_hbm) | copy-start | bytes 2359300
  3.2 1.0 %copy-start.1 = (bf16[2,128,1024]{2,1,0:T(8,128)(2,1)S(1)}, bf16[2,128,1024]{2,1,0:T(8,128)(2,1)}, u32[]{:S(2)}) copy-start(bf16[2,128,1024]{2,1,0:T(8,128)(2,1)} %constant.10.clone.column_hbm) | copy-start | bytes 1572868

commit v2 on v1

--- a/solution.py
+++ b/solution.py
@@ -51,7 +51,7 @@
     out_ref, twiddle, pick, column, amp, left, send_f, send_a, recv_f, recv_a,
     load_sem, sent_f, sent_a, got_f, got_a,
 ):
-    layers, _, sources, comps, depth = adj_ref.shape
+    layers, sources, comps, _, depth = adj_ref.shape
     n_dev = n_harm * n_tile
     wide = amp.shape[-1]
     harm = lax.axis_index("harm")
@@ -82,12 +82,15 @@
     mine = jnp.int32(0)
     for layer in range(1, layers):
         mine = jnp.where(owner_ref[layer] == tile, layer, mine)
-    for part in range(2):
-        for source in range(sources):
-            rows = slice(source * comps, source * comps + comps)
-            amp[0, part, rows, :depth] = fwd_ref[0, mine, part, source_ref[source]].astype(jnp.float32)
-            for layer in range(layers):
-                amp[1 + layer, part, rows, :depth] = adj_ref[layer, part, source].astype(jnp.float32)
+    for source in range(sources):
+        for comp in range(comps):
+            row = source * comps + comp
+            lines = [fwd_ref[0, mine, source_ref[source], comp]]
+            lines += [adj_ref[layer, source, comp] for layer in range(layers)]
+            for group, line in enumerate(lines):
+                line = line.astype(jnp.float32)
+                for part in range(2):
+                    amp[group, part, row : row + 1, :depth] = line[part : part + 1]
     loads[0].wait()
     loads[1].wait()
 
@@ -229,7 +232,9 @@
     slots = n_tile + layers
     vmem = pl.BlockSpec(memory_space=pltpu.VMEM)
     smem = pl.BlockSpec(memory_space=pltpu.SMEM)
-    hbm = pl.BlockSpec(memory_space=pl.ANY)
+    hbm = pl.BlockSpec(memory_space=pltpu.HBM)
+    fwd_ckpt = jnp.transpose(fwd_ckpt, (0, 1, 3, 4, 2, 5))
+    adj_amp = jnp.transpose(adj_amp, (0, 2, 3, 1, 4))
     total = pl.pallas_call(
         functools.partial(kernel, n_harm, n_tile),
         out_shape=jax.ShapeDtypeStruct((layers, GRID), jnp.float32),
@@ -252,7 +257,7 @@
             pltpu.SemaphoreType.DMA((n_harm,)),
         ],
         compiler_params=pltpu.CompilerParams(
-            collective_id=0, has_side_effects=True, vmem_limit_bytes=40 * 1024 * 1024
+            collective_id=0, has_side_effects=True, vmem_limit_bytes=63 * 1024 * 1024
         ),
     )(
         fwd_ckpt, adj_amp, layer_owner, source_list,

time: 19.6 us -> 16.6 us (0.85)
  local copies, waits for them, and re-layouts: 4.16 us -> 0 us
  other arithmetic: 0.6 us -> 1.28 us
  Pallas kernels: 14.5 us -> 15.1 us
    unnamed x12 -> x0, local copies, waits for them, and re-layouts: 4.16 us -> none
    mul x1, other arithmetic: 0.6 us -> 1.28 us  [per_device(): return total * jnp.float32((sources * comps) ** (-0.5))]
    pallas_call x1, Pallas kernels: 14.5 us -> 15.1 us  [per_device(): pl.pallas_call(functools.partial(kernel, n_harm, n_tile), out_shape=jax.S...]
where the time goes in v2:
time: 16.6 us; the launch traced here: 16.4 us
  Pallas kernels  15.1 us (91%)
  other arithmetic  1.28 us (8%)
    pallas_call x1, Pallas kernels, per_device(): pl.pallas_call(functools.partial(kernel, n_harm, n_tile), out_shape=jax.S...  15.1 us
    mul x1, other arithmetic, per_device(): return total * jnp.float32((sources * comps) ** (-0.5))  1.28 us

profile of v2, /device:TPU:0, one launch (start us, length us, event | category | flops | bytes accessed | tf_op | source)
XLA Modules:
  0.0 16.4 jit_solution(17018959886309745416)
XLA Ops:
  0.0 15.1 %shard_map.73 = f32[2,512]{1,0:T(2,128)} custom-call(bf16[1,2,6,3,2,656]{5,4,3,2,1,0:T(2,128)(2,1)} %bitcast.2, bf16[2,6,3,2,656]{4,3,2,1,0:T(2,128)(2,1)} %bitcast.3, s32[2]{0:T(128)} %owner_ref.1, s32[6]{0:T(128)} %source_ref.1, f32[4,16,2,768]{3,2,1,0:T(2,128)} %constant.8.clone.twiddle_hbm, bf16[4,768,128]{2,1,0:T(8,128)(2,1)} %constant.9.clone.pick_hbm, ...), custom_call_target="tpu_custom_call" | custom-call | tf_op jit(solution)/shard_map/pallas_call | solution.py:238
  15.1 1.3 %broadcast_multiply_fusion = f32[2,512]{1,0:T(2,128)} fusion(f32[2,512]{1,0:T(2,128)} %shard_map.73), kind=kLoop, calls=%fused_computation | loop fusion | flops 1024 | bytes 8192 | tf_op jit(solution)/shard_map/mul | solution.py:266

commit v3 on v2

--- a/solution.py
+++ b/solution.py
@@ -46,9 +46,17 @@
     return twiddle, pick, np.stack(split(column))
 
 
+def loop(first, end, body):
+    if end - first <= 16:
+        for step in range(first, end):
+            body(step)
+    else:
+        lax.fori_loop(first, end, lambda step, carry: (body(step), carry)[1], 0)
+
+
 def kernel(
-    n_harm, n_tile, fwd_ref, adj_ref, owner_ref, source_ref, twiddle_hbm, pick_hbm, column_hbm,
-    out_ref, twiddle, pick, column, amp, left, send_f, send_a, recv_f, recv_a,
+    n_harm, n_tile, fwd_hbm, adj_hbm, owner_hbm, source_hbm, twiddle_hbm, pick_hbm, column_hbm,
+    out_ref, fwd_ref, adj_ref, owner_ref, source_ref, twiddle, pick, column, amp, left, send_f, send_a, recv_f, recv_a,
     load_sem, sent_f, sent_a, got_f, got_a,
 ):
     layers, sources, comps, _, depth = adj_ref.shape
@@ -58,27 +66,37 @@
     tile = lax.axis_index("tile")
     me = harm * n_tile + tile
 
+    def peer(step):
+        other = lax.rem(me + step, n_dev)
+        return other, {"harm": other // n_tile, "tile": lax.rem(other, n_tile)}
+
+    barrier = pltpu.get_barrier_semaphore()
+
+    def greet(step):
+        pl.semaphore_signal(barrier, inc=1, device_id=peer(step)[1], device_id_type=MESH)
+
+    loop(1, n_dev, greet)
+
     loads = [
-        pltpu.make_async_copy(twiddle_hbm.at[harm], twiddle, load_sem.at[0]),
-        pltpu.make_async_copy(pick_hbm.at[harm], pick, load_sem.at[1]),
-        pltpu.make_async_copy(column_hbm, column, load_sem.at[2]),
+        pltpu.make_async_copy(source, target, load_sem.at[index])
+        for index, (source, target) in enumerate(
+            [
+                (owner_hbm, owner_ref),
+                (source_hbm, source_ref),
+                (fwd_hbm, fwd_ref),
+                (adj_hbm, adj_ref),
+                (twiddle_hbm.at[harm], twiddle),
+                (pick_hbm.at[harm], pick),
+                (column_hbm, column),
+            ]
+        )
     ]
     for load in loads:
         load.start()
 
-    def peer(step):
-        other = lax.rem(me + step, n_dev)
-        return other, {"harm": other // n_tile, "tile": lax.rem(other, n_tile)}
-
-    barrier = pltpu.get_barrier_semaphore()
-
-    def greet(step, carry):
-        pl.semaphore_signal(barrier, inc=1, device_id=peer(step)[1], device_id_type=MESH)
-        return carry
-
-    lax.fori_loop(1, n_dev, greet, 0)
-
     amp[...] = jnp.zeros_like(amp)
+    for load in loads[:4]:
+        load.wait()
     mine = jnp.int32(0)
     for layer in range(1, layers):
         mine = jnp.where(owner_ref[layer] == tile, layer, mine)
@@ -91,8 +109,8 @@
                 line = line.astype(jnp.float32)
                 for part in range(2):
                     amp[group, part, row : row + 1, :depth] = line[part : part + 1]
-    loads[0].wait()
-    loads[1].wait()
+    loads[4].wait()
+    loads[5].wait()
 
     low_lanes = lax.broadcasted_iota(jnp.int32, (ROWS, LANES), 1) < HALF
 
@@ -148,8 +166,8 @@
     def compute(to_harm):
         fwd, adj = partial_sums(to_harm)
         for to_tile in range(n_tile):
-            send_f[to_harm * n_tile + to_tile] = fwd[to_tile]
-        send_a[to_harm] = jnp.concatenate(adj, axis=0)
+            send_f[to_harm * n_tile + to_tile] = fwd[to_tile].astype(jnp.bfloat16)
+        send_a[to_harm] = jnp.concatenate(adj, axis=0).astype(jnp.bfloat16)
 
     def block(step):
         to_harm = lax.rem(harm + step, n_harm)
@@ -165,45 +183,39 @@
     pl.semaphore_wait(barrier, n_dev - 1)
     send_block(first)
 
-    def away(step, carry):
-        send_block(block(step))
-        return carry
-
-    lax.fori_loop(2, n_harm, away, 0)
+    loop(2, n_harm, lambda step: send_block(block(step)))
 
     compute(harm)
     for step in range(1, n_tile):
         copy_f(harm, lax.rem(tile + step, n_tile), me).start()
     recv_f[me] = send_f[me]
     recv_a[harm] = send_a[harm]
-    loads[2].wait()
-
-    def arrive_f(step, carry):
+    loads[6].wait()
+
+    def arrive_f(step):
         other, _ = peer(step)
         copy_f(other // n_tile, lax.rem(other, n_tile), other).wait()
-        return carry
-
-    def arrive_a(step, carry):
+
+    def arrive_a(step):
         other = lax.rem(harm + step, n_harm)
         copy_a(other, other).wait()
-        return carry
-
-    lax.fori_loop(1, n_dev, arrive_f, 0)
-    lax.fori_loop(1, n_harm, arrive_a, 0)
+
+    loop(1, n_dev, arrive_f)
+    loop(1, n_harm, arrive_a)
 
     def add_f(layer):
         owner = owner_ref[layer]
         return lax.fori_loop(
             0,
             n_harm,
-            lambda source, total: total + recv_f[source * n_tile + owner],
+            lambda source, total: total + recv_f[source * n_tile + owner].astype(jnp.float32),
             jnp.zeros((ROWS, LANES), jnp.float32),
         )
 
     adj = lax.fori_loop(
         0,
         n_harm,
-        lambda source, total: total + recv_a[source],
+        lambda source, total: total + recv_a[source].astype(jnp.float32),
         jnp.zeros((layers * ROWS, LANES), jnp.float32),
     )
     lines = jnp.concatenate([add_f(layer) for layer in range(layers)] + [adj], axis=0)
@@ -231,26 +243,29 @@
     twiddle, pick, column = make_tables(n_harm, n_tile, depth, wide)
     slots = n_tile + layers
     vmem = pl.BlockSpec(memory_space=pltpu.VMEM)
-    smem = pl.BlockSpec(memory_space=pltpu.SMEM)
     hbm = pl.BlockSpec(memory_space=pltpu.HBM)
     fwd_ckpt = jnp.transpose(fwd_ckpt, (0, 1, 3, 4, 2, 5))
     adj_amp = jnp.transpose(adj_amp, (0, 2, 3, 1, 4))
     total = pl.pallas_call(
         functools.partial(kernel, n_harm, n_tile),
         out_shape=jax.ShapeDtypeStruct((layers, GRID), jnp.float32),
-        in_specs=[vmem, vmem, smem, smem, hbm, hbm, hbm],
+        in_specs=[hbm] * 7,
         out_specs=vmem,
         scratch_shapes=[
+            pltpu.VMEM(fwd_ckpt.shape, jnp.bfloat16),
+            pltpu.VMEM(adj_amp.shape, jnp.bfloat16),
+            pltpu.SMEM(layer_owner.shape, jnp.int32),
+            pltpu.SMEM(source_list.shape, jnp.int32),
             pltpu.VMEM((n_dev, 2, wide), jnp.float32),
             pltpu.VMEM((wide, LANES), jnp.bfloat16),
             pltpu.VMEM(column.shape, jnp.bfloat16),
             pltpu.VMEM((1 + layers, 2, ROWS, wide), jnp.float32),
             pltpu.VMEM((2, slots * 2 * ROWS, wide), jnp.bfloat16),
-            pltpu.VMEM((n_dev, ROWS, LANES), jnp.float32),
-            pltpu.VMEM((n_harm, layers * ROWS, LANES), jnp.float32),
-            pltpu.VMEM((n_dev, ROWS, LANES), jnp.float32),
-            pltpu.VMEM((n_harm, layers * ROWS, LANES), jnp.float32),
-            pltpu.SemaphoreType.DMA((3,)),
+            pltpu.VMEM((n_dev, ROWS, LANES), jnp.bfloat16),
+            pltpu.VMEM((n_harm, layers * ROWS, LANES), jnp.bfloat16),
+            pltpu.VMEM((n_dev, ROWS, LANES), jnp.bfloat16),
+            pltpu.VMEM((n_harm, layers * ROWS, LANES), jnp.bfloat16),
+            pltpu.SemaphoreType.DMA((7,)),
             pltpu.SemaphoreType.DMA((n_dev,)),
             pltpu.SemaphoreType.DMA((n_harm,)),
             pltpu.SemaphoreType.DMA((n_dev,)),

time: 16.6 us -> 13.3 us (0.80)
  Pallas kernels: 15.1 us -> 11.9 us
    pallas_call x1, Pallas kernels: 15.1 us -> 11.9 us  [per_device(): pl.pallas_call(functools.partial(kernel, n_harm, n_tile), out_shape=jax.S...]
where the time goes in v3:
time: 13.3 us; the launch traced here: 13.1 us
  Pallas kernels  11.9 us (89%)
  other arithmetic  1.28 us (10%)
    pallas_call x1, Pallas kernels, per_device(): pl.pallas_call(functools.partial(kernel, n_harm, n_tile), out_shape=jax.S...  11.9 us
    mul x1, other arithmetic, per_device(): return total * jnp.float32((sources * comps) ** (-0.5))  1.28 us

profile of v3, /device:TPU:0, one launch (start us, length us, event | category | flops | bytes accessed | tf_op | source)
XLA Modules:
  0.0 13.1 jit_solution(16912155891851472896)
XLA Ops:
  0.0 11.9 %shard_map.73 = f32[2,512]{1,0:T(2,128)} custom-call(bf16[1,2,6,3,2,656]{5,4,3,2,1,0:T(2,128)(2,1)} %bitcast.2, bf16[2,6,3,2,656]{4,3,2,1,0:T(2,128)(2,1)} %bitcast.3, s32[2]{0:T(128)} %owner_hbm.1, s32[6]{0:T(128)} %source_hbm.1, f32[4,16,2,768]{3,2,1,0:T(2,128)} %constant.8.clone.twiddle_hbm, bf16[4,768,128]{2,1,0:T(8,128)(2,1)} %constant.9.clone.pick_hbm, ...), custom_call_target="tpu_custom_call" | custom-call | tf_op jit(solution)/shard_map/pallas_call | solution.py:249
  11.9 1.3 %broadcast_multiply_fusion = f32[2,512]{1,0:T(2,128)} fusion(f32[2,512]{1,0:T(2,128)} %shard_map.73), kind=kLoop, calls=%fused_computation | loop fusion | flops 1024 | bytes 8192 | tf_op jit(solution)/shard_map/mul | solution.py:281

commit v4 on v3

--- a/solution.py
+++ b/solution.py
@@ -272,11 +272,16 @@
             pltpu.SemaphoreType.DMA((n_harm,)),
         ],
         compiler_params=pltpu.CompilerParams(
-            collective_id=0, has_side_effects=True, vmem_limit_bytes=63 * 1024 * 1024
+            collective_id=0, has_side_effects=True, vmem_limit_bytes=24 * 1024 * 1024
         ),
     )(
-        fwd_ckpt, adj_amp, layer_owner, source_list,
-        jnp.asarray(twiddle), jnp.asarray(pick), jnp.asarray(column),
+        *[
+            pltpu.with_memory_space_constraint(value, pltpu.HBM)
+            for value in (
+                fwd_ckpt, adj_amp, layer_owner, source_list,
+                jnp.asarray(twiddle), jnp.asarray(pick), jnp.asarray(column),
+            )
+        ]
     )
     return total * jnp.float32((sources * comps) ** (-0.5))
 

time: 13.3 us -> 12 us (0.902)
  Pallas kernels: 11.9 us -> 11.2 us
  other arithmetic: 1.28 us -> 0.6 us
    mul x1, other arithmetic: 1.28 us -> 0.6 us  [per_device(): return total * jnp.float32((sources * comps) ** (-0.5))]
    pallas_call x1, Pallas kernels: 11.9 us -> 11.2 us  [per_device(): pl.pallas_call(functools.partial(kernel, n_harm, n_tile), out_shape=jax.S...]
where the time goes in v4:
time: 12 us; the launch traced here: 11.8 us
  Pallas kernels  11.2 us (93%)
  other arithmetic  0.6 us (5%)
    pallas_call x1, Pallas kernels, per_device(): pl.pallas_call(functools.partial(kernel, n_harm, n_tile), out_shape=jax.S...  11.2 us
    mul x1, other arithmetic, per_device(): return total * jnp.float32((sources * comps) ** (-0.5))  0.6 us

profile of v4, /device:TPU:0, one launch (start us, length us, event | category | flops | bytes accessed | tf_op | source)
XLA Modules:
  0.0 11.8 jit_solution(3274306020306441577)
XLA Ops:
  0.0 11.2 %shard_map.73 = f32[2,512]{1,0:T(2,128)S(1)} custom-call(bf16[1,2,6,3,2,656]{5,4,3,2,1,0:T(2,128)(2,1)} %bitcast.2, bf16[2,6,3,2,656]{4,3,2,1,0:T(2,128)(2,1)} %bitcast.3, s32[2]{0:T(128)} %owner_hbm.1, s32[6]{0:T(128)} %source_hbm.1, f32[4,16,2,768]{3,2,1,0:T(2,128)} %constant.8.clone.twiddle_hbm, bf16[4,768,128]{2,1,0:T(8,128)(2,1)} %constant.9.clone.pick_hbm, ...), custom_call_target="tpu_custom_call" | custom-call | tf_op jit(solution)/shard_map/pallas_call | solution.py:249
  11.3 0.6 %broadcast_multiply_fusion = f32[2,512]{1,0:T(2,128)} fusion(f32[2,512]{1,0:T(2,128)S(1)} %shard_map.73), kind=kLoop, calls=%fused_computation | loop fusion | flops 1024 | bytes 8192 | tf_op jit(solution)/shard_map/mul | solution.py:286

commit v5 on v4

--- a/solution.py
+++ b/solution.py
@@ -167,7 +167,11 @@
         fwd, adj = partial_sums(to_harm)
         for to_tile in range(n_tile):
             send_f[to_harm * n_tile + to_tile] = fwd[to_tile].astype(jnp.bfloat16)
-        send_a[to_harm] = jnp.concatenate(adj, axis=0).astype(jnp.bfloat16)
+        lines = [one[: sources * comps] for one in adj]
+        spare = send_a.shape[1] - layers * sources * comps
+        if spare:
+            lines.append(jnp.zeros((spare, LANES), jnp.float32))
+        send_a[to_harm] = jnp.concatenate(lines, axis=0).astype(jnp.bfloat16)
 
     def block(step):
         to_harm = lax.rem(harm + step, n_harm)
@@ -175,9 +179,9 @@
         return to_harm
 
     def send_block(to_harm):
+        copy_a(to_harm, harm).start()
         for to_tile in range(n_tile):
             copy_f(to_harm, to_tile, me).start()
-        copy_a(to_harm, harm).start()
 
     first = block(1)
     pl.semaphore_wait(barrier, n_dev - 1)
@@ -203,21 +207,21 @@
     loop(1, n_dev, arrive_f)
     loop(1, n_harm, arrive_a)
 
-    def add_f(layer):
-        owner = owner_ref[layer]
+    def add(part, shape):
+        if n_harm <= 16:
+            return sum(part(source).astype(jnp.float32) for source in range(n_harm))
         return lax.fori_loop(
             0,
             n_harm,
-            lambda source, total: total + recv_f[source * n_tile + owner].astype(jnp.float32),
-            jnp.zeros((ROWS, LANES), jnp.float32),
-        )
-
-    adj = lax.fori_loop(
-        0,
-        n_harm,
-        lambda source, total: total + recv_a[source].astype(jnp.float32),
-        jnp.zeros((layers * ROWS, LANES), jnp.float32),
-    )
+            lambda source, total: total + part(source).astype(jnp.float32),
+            jnp.zeros(shape, jnp.float32),
+        )
+
+    def add_f(layer):
+        owner = owner_ref[layer]
+        return add(lambda source: recv_f[source * n_tile + owner], (ROWS, LANES))
+
+    adj = add(lambda source: recv_a[source], recv_a.shape[1:])
     lines = jnp.concatenate([add_f(layer) for layer in range(layers)] + [adj], axis=0)
     high = lines.astype(jnp.bfloat16)
     low = (lines - high.astype(jnp.float32)).astype(jnp.bfloat16)
@@ -227,8 +231,9 @@
         + jnp.dot(high, column[1], preferred_element_type=jnp.float32)
     )
     for layer in range(layers):
-        one = fields[layer * ROWS : (layer + 1) * ROWS]
-        two = fields[(layers + layer) * ROWS : (layers + layer + 1) * ROWS]
+        rows = sources * comps
+        one = fields[layer * ROWS : layer * ROWS + rows]
+        two = fields[layers * ROWS + layer * rows : layers * ROWS + (layer + 1) * rows]
         both = one * two
         out_ref[layer : layer + 1, :] = jnp.sum(
             both[:, :GRID] - both[:, GRID:], axis=0, keepdims=True
@@ -262,9 +267,9 @@
             pltpu.VMEM((1 + layers, 2, ROWS, wide), jnp.float32),
             pltpu.VMEM((2, slots * 2 * ROWS, wide), jnp.bfloat16),
             pltpu.VMEM((n_dev, ROWS, LANES), jnp.bfloat16),
-            pltpu.VMEM((n_harm, layers * ROWS, LANES), jnp.bfloat16),
+            pltpu.VMEM((n_harm, -(-layers * sources * comps // 8) * 8, LANES), jnp.bfloat16),
             pltpu.VMEM((n_dev, ROWS, LANES), jnp.bfloat16),
-            pltpu.VMEM((n_harm, layers * ROWS, LANES), jnp.bfloat16),
+            pltpu.VMEM((n_harm, -(-layers * sources * comps // 8) * 8, LANES), jnp.bfloat16),
             pltpu.SemaphoreType.DMA((7,)),
             pltpu.SemaphoreType.DMA((n_dev,)),
             pltpu.SemaphoreType.DMA((n_harm,)),

time: 12 us -> 11.7 us (0.975)
  Pallas kernels: 11.2 us -> 10.9 us
    pallas_call x1, Pallas kernels: 11.2 us -> 10.9 us  [per_device(): pl.pallas_call(functools.partial(kernel, n_harm, n_tile), out_shape=jax.S...]
where the time goes in v5:
time: 11.7 us; the launch traced here: 11.6 us
  Pallas kernels  10.9 us (93%)
  other arithmetic  0.6 us (5%)
    pallas_call x1, Pallas kernels, per_device(): pl.pallas_call(functools.partial(kernel, n_harm, n_tile), out_shape=jax.S...  10.9 us
    mul x1, other arithmetic, per_device(): return total * jnp.float32((sources * comps) ** (-0.5))  0.6 us

profile of v5, /device:TPU:0, one launch (start us, length us, event | category | flops | bytes accessed | tf_op | source)
XLA Modules:
  0.0 11.6 jit_solution(15337086576048343981)
XLA Ops:
  0.0 10.9 %shard_map.73 = f32[2,512]{1,0:T(2,128)S(1)} custom-call(bf16[1,2,6,3,2,656]{5,4,3,2,1,0:T(2,128)(2,1)} %bitcast.2, bf16[2,6,3,2,656]{4,3,2,1,0:T(2,128)(2,1)} %bitcast.3, s32[2]{0:T(128)} %owner_hbm.1, s32[6]{0:T(128)} %source_hbm.1, f32[4,16,2,768]{3,2,1,0:T(2,128)} %constant.8.clone.twiddle_hbm, bf16[4,768,128]{2,1,0:T(8,128)(2,1)} %constant.9.clone.pick_hbm, ...), custom_call_target="tpu_custom_call" | custom-call | tf_op jit(solution)/shard_map/pallas_call | solution.py:254
  11.0 0.6 %broadcast_multiply_fusion = f32[2,512]{1,0:T(2,128)} fusion(f32[2,512]{1,0:T(2,128)S(1)} %shard_map.73), kind=kLoop, calls=%fused_computation | loop fusion | flops 1024 | bytes 8192 | tf_op jit(solution)/shard_map/mul | solution.py:291
